TPU v7x, 512 devices: a whole 4x4x16 slice. The times are simulated.
512 devices in a mesh: dp: 32 (over z, core), mp: 16 (over x, y).
Axes of the slice: x: 4, y: 4, z: 16, core: 2. Of those that a mesh axis runs over, the one named last changes fastest.
Arguments:
- tokens: bfloat16 [4096, 4096], P('dp', 'mp'), may hold values from -55 to 55
- encodings: bfloat16 [16384, 896], P('dp'), may hold values from -6 to 6
- shard_place: int32 [32, 512], P('dp'), may hold values from 0 to 511, each once within a row
- owner_map: int32 [32, 512], P('dp'), may hold values from 0 to 511, each once within a row
- query_weight: bfloat16 [4096, 2048], P('dp', 'mp'), may hold values from -0.09375 to 0.09375
- key_weight: bfloat16 [896, 2048], P('dp', 'mp'), may hold values from -0.1875 to 0.1875
- value_weight: bfloat16 [896, 2048], P('dp', 'mp'), may hold values from -0.1875 to 0.1875
- out_weight: bfloat16 [2048, 4096], P('mp', 'dp'), may hold values from -0.125 to 0.125
- grad_out: bfloat16 [4096, 4096], P('dp', 'mp'), may hold values from -6 to 6
Outputs:
- layer_out: bfloat16 [4096, 4096], P('dp')
- input_grad: bfloat16 [4096, 4096], P('dp', 'mp')
- query_grad: bfloat16 [4096, 2048], P('dp', 'mp')
- key_grad: bfloat16 [896, 2048], P('dp', 'mp')
- value_grad: bfloat16 [896, 2048], P('dp', 'mp')
- out_grad: bfloat16 [2048, 4096], P('mp', 'dp')
- encoding_grad: bfloat16 [16384, 896], P('dp')
Inputs may be any that keep to these rules, and one draw needn't show every extreme that they name: `shard_place`: each row is an ordering of 0 to 511. `owner_map`: each row is an ordering of 0 to 511.
All inputs are finite; a program needn't handle non-finite values.
Results may differ from a plain program's by a relative error of at most 0.034.
Values may be sent and summed in bfloat16 or wider, within the bound.
A program may use at most 64 MiB of HBM per device.

v0:
```python
import jax
import jax.numpy as jnp
from jax import lax
from jax.sharding import PartitionSpec as P

HDIM = 128
STRETCH = 64
NEIGH = 2
NLEN = 128
SEQ_LEN = 2048


def shifted(block, axis, distance):
    devices = range(lax.axis_size(axis))
    route = [(i - distance, i) for i in devices if i - distance in devices]
    return lax.ppermute(block, axis, route)


def slot_mask(device, block_count, token_count):
    slot_ids = jnp.arange(block_count, dtype=jnp.int32)[:, None]
    local_pos = slot_ids * STRETCH - 1 + jnp.arange(STRETCH, dtype=jnp.int32)[None, :]
    token_pos = device * token_count + local_pos
    stretch_start = (device * (block_count - 1) + slot_ids - 1) * STRETCH
    return (
        (local_pos >= 0)
        & (local_pos < token_count)
        & (token_pos // SEQ_LEN == stretch_start // SEQ_LEN)
    )


def softmax_rows(scores):
    row_top = jnp.max(scores, -1, keepdims=True)
    expo_terms = jnp.exp(scores - row_top)
    return expo_terms / jnp.sum(expo_terms, -1, keepdims=True)


def sum_heads(row_grads, projection):
    head_part = jnp.einsum("rc,ec->re", row_grads, projection, preferred_element_type=jnp.float32)
    return lax.psum(head_part.astype(jnp.bfloat16), "mp")


def shards(
    tokens,
    encodings,
    shard_place,
    owner_map,
    query_weight,
    key_weight,
    value_weight,
    out_weight,
    grad_out,
):
    score_scale = HDIM ** (-0.5)
    device = lax.axis_index("dp")
    peer_count = lax.axis_size("dp")
    row_count = encodings.shape[0]
    enc_width = encodings.shape[1]
    peer_rows = row_count // peer_count
    token_count = tokens.shape[0]
    group_cols = query_weight.shape[1]
    local_heads = group_cols // HDIM
    block_count = token_count // STRETCH + 1
    stretch_keys = NEIGH * NLEN
    send_order = shard_place[0]
    take_order = owner_map[0]
    features = lax.all_gather(tokens, "mp", axis=1, tiled=True)
    query_full = lax.all_gather(query_weight, "dp", axis=0, tiled=True)
    key_full, value_full = (
        lax.all_gather(key_weight, "dp", axis=0, tiled=True),
        lax.all_gather(value_weight, "dp", axis=0, tiled=True),
    )
    out_full = lax.all_gather(out_weight, "dp", axis=1, tiled=True)
    projection = jnp.concatenate([key_full, value_full], 1)
    queries = jnp.dot(features, query_full, preferred_element_type=jnp.float32).astype(jnp.bfloat16)
    outgoing = encodings[send_order].reshape(peer_count, peer_rows, enc_width)
    arrived = lax.all_to_all(outgoing, "dp", split_axis=0, concat_axis=0, tiled=True)
    basis_rows = arrived.reshape(row_count, enc_width)[take_order]
    key_values = jnp.dot(basis_rows, projection, preferred_element_type=jnp.float32).astype(
        jnp.bfloat16
    )
    prior_pairs = shifted(key_values[row_count - stretch_keys :], "dp", 1)
    context = jnp.concatenate([prior_pairs, key_values], 0).reshape(
        block_count, stretch_keys, 2, local_heads, HDIM
    )
    key_blocks = context[:, :, 0]
    value_blocks = context[:, :, 1]
    front_pad = jnp.zeros((1, group_cols), jnp.bfloat16)
    back_pad = jnp.zeros((STRETCH - 1, group_cols), jnp.bfloat16)
    query_blocks = jnp.concatenate([front_pad, queries, back_pad], 0).reshape(
        block_count, STRETCH, local_heads, HDIM
    )
    inside = slot_mask(device, block_count, token_count)[:, :, None, None]
    scores = (
        jnp.einsum("gqhd,gkhd->ghqk", query_blocks, key_blocks, preferred_element_type=jnp.float32)
        * score_scale
    )
    soft_probs = softmax_rows(scores)
    probs_half = soft_probs.astype(jnp.bfloat16)
    mixture = jnp.einsum(
        "ghqk,gkhd->gqhd", probs_half, value_blocks, preferred_element_type=jnp.float32
    )
    mixture = jnp.where(inside, mixture, 0.0)
    attended = mixture.astype(jnp.bfloat16).reshape(block_count * STRETCH, group_cols)[
        1 : token_count + 1
    ]
    layer_part = jnp.dot(attended, out_full, preferred_element_type=jnp.float32)
    layer_out = lax.psum(layer_part.astype(jnp.bfloat16), "mp")
    grads_in = lax.all_gather(grad_out, "mp", axis=1, tiled=True)
    query_full = lax.all_gather(query_weight, "dp", axis=0, tiled=True)
    key_full, value_full = (
        lax.all_gather(key_weight, "dp", axis=0, tiled=True),
        lax.all_gather(value_weight, "dp", axis=0, tiled=True),
    )
    out_full = lax.all_gather(out_weight, "dp", axis=1, tiled=True)
    projection = jnp.concatenate([key_full, value_full], 1)
    d_attended = jnp.einsum(
        "td,id->ti", grads_in, out_full, preferred_element_type=jnp.float32
    ).astype(jnp.bfloat16)
    out_term = jnp.einsum("ti,td->id", attended, grads_in, preferred_element_type=jnp.float32)
    out_grad = lax.psum_scatter(
        out_term.astype(jnp.bfloat16), "dp", scatter_dimension=1, tiled=True
    )
    grad_blocks = jnp.concatenate([front_pad, d_attended, back_pad], 0).reshape(
        block_count, STRETCH, local_heads, HDIM
    )
    grad_blocks = jnp.where(inside, grad_blocks, jnp.zeros((), jnp.bfloat16))
    grad_probs = jnp.einsum(
        "gqhd,gkhd->ghqk", grad_blocks, value_blocks, preferred_element_type=jnp.float32
    )
    value_terms = jnp.einsum(
        "ghqk,gqhd->gkhd", probs_half, grad_blocks, preferred_element_type=jnp.float32
    )
    grad_scores = (
        soft_probs * (grad_probs - jnp.sum(soft_probs * grad_probs, -1, keepdims=True))
    ).astype(jnp.bfloat16)
    query_terms = (
        jnp.einsum("ghqk,gkhd->gqhd", grad_scores, key_blocks, preferred_element_type=jnp.float32)
        * score_scale
    )
    key_terms = (
        jnp.einsum("ghqk,gqhd->gkhd", grad_scores, query_blocks, preferred_element_type=jnp.float32)
        * score_scale
    )
    pair_terms = jnp.stack([key_terms, value_terms], 2).reshape(
        block_count, stretch_keys, 2 * group_cols
    )
    carried = shifted(pair_terms[0], "dp", -1)
    pair_terms = pair_terms[1:].at[block_count - 2].add(carried)
    pair_grads = pair_terms.reshape(row_count, 2 * group_cols).astype(jnp.bfloat16)
    grad_queries = query_terms.astype(jnp.bfloat16).reshape(block_count * STRETCH, group_cols)[
        1 : token_count + 1
    ]
    input_term = jnp.einsum(
        "ti,di->td", grad_queries, query_full, preferred_element_type=jnp.float32
    )
    input_grad = lax.psum_scatter(
        input_term.astype(jnp.bfloat16), "mp", scatter_dimension=1, tiled=True
    )
    query_grad = lax.psum_scatter(
        jnp.einsum("td,ti->di", features, grad_queries, preferred_element_type=jnp.float32).astype(
            jnp.bfloat16
        ),
        "dp",
        scatter_dimension=0,
        tiled=True,
    )
    owner_grads = sum_heads(pair_grads, projection)
    back_rows = jnp.zeros_like(owner_grads).at[take_order].set(owner_grads)
    home_rows = lax.all_to_all(
        back_rows.reshape(peer_count, peer_rows, enc_width),
        "dp",
        split_axis=0,
        concat_axis=0,
        tiled=True,
    )
    encoding_grad = (
        jnp.zeros_like(owner_grads).at[send_order].set(home_rows.reshape(row_count, enc_width))
    )
    pair_sum = lax.psum_scatter(
        jnp.einsum("re,rc->ec", basis_rows, pair_grads, preferred_element_type=jnp.float32),
        "dp",
        scatter_dimension=0,
        tiled=True,
    )
    key_grad = pair_sum[:, :group_cols].astype(jnp.bfloat16)
    value_grad = pair_sum[:, group_cols:].astype(jnp.bfloat16)
    return (layer_out, input_grad, query_grad, key_grad, value_grad, out_grad, encoding_grad)


def solution(mesh):
    placed = (
        P("dp", "mp"),
        P("dp", None),
        P("dp", None),
        P("dp", None),
        P("dp", "mp"),
        P("dp", "mp"),
        P("dp", "mp"),
        P("mp", "dp"),
        P("dp", "mp"),
    )
    return jax.shard_map(
        shards,
        mesh=mesh,
        in_specs=placed,
        out_specs=(
            P("dp", None),
            P("dp", "mp"),
            P("dp", "mp"),
            P("dp", "mp"),
            P("dp", "mp"),
            P("mp", "dp"),
            P("dp", None),
        ),
        check_vma=False,
    )
```

profile of v0, /device:TPU:1, one launch (start us, length us, event | category | flops | bytes accessed | tf_op | source)
XLA Modules:
  0.0 750.1 jit_solution(12262767048714240383)
XLA Ops:
  10.1 2.7 gather_fusion
  12.8 16.9 %all-to-all-start = ((bf16[32,16,896]{2,1,0:T(8,128)(2,1)}), bf16[32,16,896]{2,1,0:T(8,128)(2,1)S(1)}, u32[]{:S(2)}, u32[]{:S(2)}) async-start(bf16[32,16,896]{2,1,0:T(8,128)(2,1)} %bitcast.2), calls=%async_computation | async-start | bytes 1835008 | tf_op jit(solution)/shard_map/all_to_all | solution.py:76
  30.5 66.6 %all-gather = bf16[32,28,128]{2,1,0:T(8,128)(2,1)S(1)} all-gather(bf16[1,28,128]{2,1,0:T(8,128)(2,1)S(1)} %bitcast.104), channel_id=1, replica_groups=mesh['dp'=32,'mp'=16] {'dp'}, dimensions={0}, use_global_device_ids=true | all-gather | bytes 236544 | tf_op jit(solution)/shard_map/all_gather | solution.py:69
  97.1 28.3 %all-gather.1 = bf16[32,28,128]{2,1,0:T(8,128)(2,1)S(1)} all-gather(bf16[1,28,128]{2,1,0:T(8,128)(2,1)S(1)} %bitcast.105), channel_id=1, replica_groups=mesh['dp'=32,'mp'=16] {'dp'}, dimensions={0}, use_global_device_ids=true | all-gather | bytes 236544 | tf_op jit(solution)/shard_map/all_gather | solution.py:70
  125.8 21.4 %all-gather.11.cloned.1.call-done = bf16[128,4096]{1,0:T(8,128)(2,1)} async-done(((bf16[128,128]{1,0:T(8,128)(2,1)}), bf16[128,4096]{1,0:T(8,128)(2,1)}) %all-gather.11.cloned.1.call-update) | async-done | bytes 1048592 | tf_op jit(solution)/shard_map/all_gather | solution.py:72
  147.1 2.0 convolution_convert_fusion.6
  149.1 53.8 %all-gather.7.cloned.1.call-done = bf16[128,4096]{1,0:T(8,128)(2,1)} async-done(((bf16[128,256]{1,0:T(8,128)(2,1)}), bf16[128,4096]{1,0:T(8,128)(2,1)}) %all-gather.7.cloned.1.call-update) | async-done | bytes 1048592 | tf_op jit(solution)/shard_map/all_gather | solution.py:66
  202.9 73.9 %all-gather.9.cloned.1.call-done = bf16[4096,128]{1,0:T(8,128)(2,1)} async-done(((bf16[128,128]{1,0:T(8,128)(2,1)}), bf16[4096,128]{1,0:T(8,128)(2,1)}) %all-gather.9.cloned.1.call-update) | async-done | bytes 1048592 | tf_op jit(solution)/shard_map/all_gather | solution.py:67
  276.8 2.0 convolution_convert_fusion.7
  278.8 2.1 gather_fusion.1
  281.3 3.2 collective-permute-start
  284.7 1.8 collective-permute-done
  290.4 2.1 collective-permute-start.1
  293.9 5.1 collective-permute-done.1
  306.7 110.0 %all-reduce.5.cloned.1.call-done = (bf16[128,4096]{1,0:T(8,128)(2,1)}, bf16[512,896]{1,0:T(8,128)(2,1)}) async-done(((bf16[128,4096]{1,0:T(8,128)(2,1)}, bf16[512,896]{1,0:T(8,128)(2,1)}), (bf16[128,4096]{1,0:T(8,128)(2,1)}, bf16[512,896]{1,0:T(8,128)(2,1)})) %all-reduce.5.cloned.1.call-update) | async-done | bytes 1966096 | tf_op jit(solution)/shard_map/psum | solution.py:107
  416.7 4.3 scatter_custom_fusion
  421.0 14.4 %all-to-all-start.1 = ((bf16[32,16,896]{2,1,0:T(8,128)(2,1)}), bf16[32,16,896]{2,1,0:T(8,128)(2,1)}, u32[]{:S(2)}, u32[]{:S(2)}) async-start(bf16[32,16,896]{2,1,0:T(8,128)(2,1)} %bitcast.30), calls=%async_computation.2 | async-start | bytes 1835008 | tf_op jit(solution)/shard_map/all_to_all | solution.py:169
  438.5 85.8 %fusion = f32[32,256]{1,0:T(8,128)S(1)} fusion(f32[896,256]{1,0:T(8,128)S(1)} %fusion.39), kind=kCustom, calls=%all-reduce-scatter | all-reduce-scatter fusion | flops 262145 | bytes 952320
  525.7 3.7 collective-permute-start.4
  529.4 3.3 collective-permute-start.2
  532.8 5.2 collective-permute-start.5
  542.6 4.3 scatter_custom_fusion.1
  546.9 103.5 %reduce-scatter.12.cloned.1.call-done = bf16[128,128]{1,0:T(8,128)(2,1)} async-done(((bf16[4096,128]{1,0:T(8,128)(2,1)}), bf16[128,128]{1,0:T(8,128)(2,1)}) %reduce-scatter.12.cloned.1.call-update) | async-done | bytes 32784
  650.4 92.0 %reduce-scatter.10.cloned.1.call-done = bf16[128,256]{1,0:T(8,128)(2,1)} async-done(((bf16[128,4096]{1,0:T(8,128)(2,1)}), bf16[128,256]{1,0:T(8,128)(2,1)}) %reduce-scatter.10.cloned.1.call-update) | async-done | bytes 65552 | tf_op jit(solution)/shard_map/reduce_scatter | solution.py:156
  (101 shorter events, 26.8 us)
Async XLA Ops:
  7.2 118.6 %all-gather.13.cloned.1.call-start = ((), (), s32[]{:S(2)}) async-start(), calls=%async_computation.8 | async-start | bytes 1114112 | tf_op jit(solution)/shard_map/all_gather | solution.py:108
  7.9 139.2 %all-gather.11.cloned.1.call-start = ((), (), s32[]{:S(2)}) async-start(), calls=%async_computation.7 | async-start | bytes 1081344 | tf_op jit(solution)/shard_map/all_gather | solution.py:72
  8.7 194.2 %all-gather.7.cloned.1.call-start = ((), (), s32[]{:S(2)}) async-start(), calls=%async_computation.5 | async-start | bytes 1114112 | tf_op jit(solution)/shard_map/all_gather | solution.py:66
  12.8 17.6 %copy-start.11 = (bf16[28,128]{1,0:T(8,128)(2,1)S(1)}, bf16[28,128]{1,0:T(8,128)(2,1)}, u32[]{:S(2)}) copy-start(bf16[28,128]{1,0:T(8,128)(2,1)} %param.16) | copy-start | bytes 21508
  12.8 84.3 %copy-start.12 = (bf16[28,128]{1,0:T(8,128)(2,1)S(1)}, bf16[28,128]{1,0:T(8,128)(2,1)}, u32[]{:S(2)}) copy-start(bf16[28,128]{1,0:T(8,128)(2,1)} %param.17) | copy-start | bytes 21508
  12.8 266.0 %all-to-all-start = ((bf16[32,16,896]{2,1,0:T(8,128)(2,1)}), bf16[32,16,896]{2,1,0:T(8,128)(2,1)S(1)}, u32[]{:S(2)}, u32[]{:S(2)}) async-start(bf16[32,16,896]{2,1,0:T(8,128)(2,1)} %bitcast.2), calls=%async_computation | async-start | bytes 1835008 | tf_op jit(solution)/shard_map/all_to_all | solution.py:76
  29.7 95.8 %copy-start.13 = (s32[1,512]{1,0:T(1,128)S(1)}, s32[1,512]{1,0:T(1,128)}, u32[]{:S(2)}) copy-start(s32[1,512]{1,0:T(1,128)} %param.14) | copy-start | bytes 6148
  29.7 247.1 %all-gather.9.cloned.1.call-start = ((), (), s32[]{:S(2)}) async-start(), calls=%async_computation.6 | async-start | bytes 1081344 | tf_op jit(solution)/shard_map/all_gather | solution.py:67
  30.3 386.4 %all-reduce.5.cloned.1.call-start = ((), (), s32[]{:S(2)}) async-start(), calls=%async_computation.12 | async-start | bytes 3932160 | tf_op jit(solution)/shard_map/psum | solution.py:107
  125.7 155.2 %copy-start.8 = (bf16[896,256]{1,0:T(8,128)(2,1)}, bf16[896,256]{1,0:T(8,128)(2,1)S(1)}, u32[]{:S(2)}) copy-start(bf16[896,256]{1,0:T(8,128)(2,1)S(1)} %constant_dynamic-update-slice_fusion) | copy-start | bytes 1376260
  280.9 3.8 copy-start.5
  281.3 5.1 collective-permute-start
  290.4 8.5 %collective-permute-start.1 = (f32[256,256]{0,1:T(8,128)S(1)}, f32[256,256]{0,1:T(8,128)S(1)}, u32[]{:S(2)}, u32[]{:S(2)}) collective-permute-start(f32[256,256]{0,1:T(8,128)S(1)} %bitcast.96), channel_id=1, source_target_pairs={{16,0},{32,16},{48,32},{64,48},{80,64},{96,80},{112,96},{128,112},... | collective-permute-start | bytes 786440 | tf_op jit(solution)/shard_map/ppermute | solution.py:16
  293.9 5.2 copy-start.9
  300.6 240.6 %reduce-scatter.14.cloned.1.call-start = ((), (), s32[]{:S(2)}) async-start(), calls=%async_computation.11 | async-start | bytes 1081344
  303.6 346.8 %reduce-scatter.12.cloned.1.call-start = ((), (), s32[]{:S(2)}) async-start(), calls=%async_computation.10 | async-start | bytes 1081344
  421.0 14.4 %copy-start.1 = (bf16[4096,128]{1,0:T(8,128)(2,1)S(1)}, bf16[4096,128]{1,0:T(8,128)(2,1)}, u32[]{:S(2)}) copy-start(bf16[4096,128]{1,0:T(8,128)(2,1)} %all-gather.9.cloned.1.call-done) | copy-start | bytes 3145732
  421.0 121.6 %all-to-all-start.1 = ((bf16[32,16,896]{2,1,0:T(8,128)(2,1)}), bf16[32,16,896]{2,1,0:T(8,128)(2,1)}, u32[]{:S(2)}, u32[]{:S(2)}) async-start(bf16[32,16,896]{2,1,0:T(8,128)(2,1)} %bitcast.30), calls=%async_computation.2 | async-start | bytes 1835008 | tf_op jit(solution)/shard_map/all_to_all | solution.py:169
  435.4 307.0 %reduce-scatter.10.cloned.1.call-start = ((), (), s32[]{:S(2)}) async-start(), calls=%async_computation.9 | async-start | bytes 1114112 | tf_op jit(solution)/shard_map/reduce_scatter | solution.py:156
  524.3 218.1 %copy-start.7 = (bf16[128,4096]{1,0:T(8,128)(2,1)S(1)}, bf16[128,4096]{1,0:T(8,128)(2,1)}, u32[]{:S(2)}) copy-start(bf16[128,4096]{1,0:T(8,128)(2,1)} %get-tuple-element.59) | copy-start | bytes 3145732
  524.3 15.6 %collective-permute-start.3 = (bf16[32,256]{1,0:T(8,128)(2,1)S(1)}, bf16[32,256]{1,0:T(8,128)(2,1)S(1)}, u32[]{:S(2)}, u32[]{:S(2)}) collective-permute-start(bf16[32,256]{1,0:T(8,128)(2,1)S(1)} %convert.14), channel_id=1, source_target_pairs={{0,32},{16,48},{32,64},{48,80},{64,96},{80,112},{96,128},{112,144}... | collective-permute-start | bytes 49160
  525.7 14.1 %collective-permute-start.4 = (bf16[32,256]{1,0:T(8,128)(2,1)S(1)}, bf16[32,256]{1,0:T(8,128)(2,1)S(1)}, u32[]{:S(2)}, u32[]{:S(2)}) collective-permute-start(bf16[32,256]{1,0:T(8,128)(2,1)S(1)} %convert.14), channel_id=1, source_target_pairs={{0,48},{16,64},{32,80},{48,96},{64,112},{80,128},{96,144},{112,160... | collective-permute-start | bytes 49160
  529.4 10.5 %collective-permute-start.2 = (bf16[32,256]{1,0:T(8,128)(2,1)S(1)}, bf16[32,256]{1,0:T(8,128)(2,1)S(1)}, u32[]{:S(2)}, u32[]{:S(2)}) collective-permute-start(bf16[32,256]{1,0:T(8,128)(2,1)S(1)} %convert.14), channel_id=1, source_target_pairs={{0,16},{16,32},{32,48},{48,64},{64,80},{80,96},{96,112},{112,128},... | collective-permute-start | bytes 49160
  532.8 7.1 collective-permute-start.5
  (6 other events, 9.6 us)
Sparse Core Ops, SparseCore 0:
  11.0 62.5 all-gather.12
  75.7 71.4 all-gather.10
  150.1 52.7 all-gather.6
  204.9 71.9 all-gather.8
  300.7 115.9 all-reduce.4
  419.3 119.2 reduce-scatter.13
  542.3 108.0 reduce-scatter.11
  655.0 87.2 reduce-scatter.9
where the time goes:
time: 752 us; the launch traced here: 750 us
  waiting for transfers between devices  464 us (62%)
  blocking collectives  181 us (24%)
  starting transfers between devices  50.4 us (7%)
  local copies, waits for them, and re-layouts  25.1 us (3%)
  between operations  15.3 us (2%)
  matrix products  12.9 us (2%)
    psum x1, waiting for transfers between devices, shards(): layer_out = lax.psum(layer_part.astype(jnp.bfloat16), 'mp')  110 us
    unnamed x14, waiting for transfers between devices  106 us
    reduce_scatter x1, waiting for transfers between devices, shards(): lax.psum_scatter(input_term.astype(jnp.bfloat16), 'mp', scatter_dimension...  92 us
    unnamed x1, blocking collectives  85.8 us
    all_gather x1, waiting for transfers between devices, shards(): query_full = lax.all_gather(query_weight, 'dp', axis=0, tiled=True)  73.9 us
    all_gather x1, blocking collectives, shards(): lax.all_gather(key_weight, 'dp', axis=0, tiled=True)  66.6 us
    all_gather x1, waiting for transfers between devices, shards(): features = lax.all_gather(tokens, 'mp', axis=1, tiled=True)  53.8 us
    all_gather x1, blocking collectives, shards(): lax.all_gather(value_weight, 'dp', axis=0, tiled=True)  28.3 us
  transfers between devices with their start and end apart: 16, of which 8 were waited for; matrix products, arithmetic and copies ran while one was open for 15% of the time, Pallas kernels for 0%

commit v1 on v0

v1 whole, which is shorter than its diff:
```python
import jax
import jax.numpy as jnp
from jax import lax
from jax.experimental import pallas as pl
from jax.experimental.pallas import tpu as pltpu
from jax.sharding import PartitionSpec as P

HDIM = 128
ENC = 896
SHARD_ROWS = 28
PAD_ROWS = 32
SCALE = HDIM ** (-0.5)
BF = jnp.bfloat16
F32 = jnp.float32
N_SEMS = 256
MESH = pl.DeviceIdType.MESH


def dot(a, b, ca=1, cb=0):
    return lax.dot_general(a, b, (((ca,), (cb,)), ((), ())), preferred_element_type=F32)


def kernel(
    tok,
    gout,
    qw,
    ow,
    kw,
    vw,
    enc,
    place,
    omap,
    layer_out,
    input_grad,
    query_grad,
    pair_grad,
    out_grad,
    enc_grad,
    feats,
    gins,
    wall,
    spread,
    sorted_enc,
    earr,
    kvs,
    lp,
    ip,
    ep,
    rs1,
    rs1e,
    rs2,
    rs2e,
    mid,
    mide,
    tz,
    tzk,
    sib,
    sibk,
    uz,
    uzk,
    rodd,
    roddk,
    rch,
    rchk,
    chs,
    chsk,
    cbuf,
    crecv,
    eout,
    hall,
    send_sems,
    recv_sems,
    local_sems,
):
    d = lax.axis_index("dp")
    m = lax.axis_index("mp")
    z, c = d // 2, d % 2
    x, y = m // 4, m % 4

    def at(dz=0, dc=0, dx=0, dy=0):
        return (((z + dz + 16) % 16) * 2 + (c + dc) % 2, ((x + dx) % 4) * 4 + (y + dy) % 4)

    count = [0]
    sent = []

    def push(src, dst, to):
        i = count[0]
        count[0] += 1
        copy = pltpu.make_async_remote_copy(
            src_ref=src,
            dst_ref=dst,
            send_sem=send_sems.at[i],
            recv_sem=recv_sems.at[i],
            device_id=to,
            device_id_type=MESH,
        )
        copy.start()
        sent.append(copy)
        return copy

    low = (m - d + 32) % 16
    self_half = jnp.where(low == d % 16, d // 16, 2)

    barrier = pltpu.get_barrier_semaphore()
    after = ((d + 1) % 32, m)
    before = ((d + 31) % 32, m)
    peers = [at(dx=k) for k in (1, 2, 3)] + [at(dy=k) for k in (1, 2, 3)]
    peers += [at(dz=k) for k in (1, -1, 2, -2)] + [at(dc=1), after, before]
    for peer in peers:
        pl.semaphore_signal(barrier, inc=1, device_id=peer, device_id_type=MESH)
    for half in range(2):
        @pl.when(self_half != half)
        def _():
            pl.semaphore_signal(barrier, inc=1, device_id=(low + 16 * half, m), device_id_type=MESH)

    for h in range(2):
        feats[x, y, h] = tok[64 * h : 64 * h + 64, :]
        gins[x, y, h] = gout[64 * h : 64 * h + 64, :]
    wall[z, c, 0:64, :] = jnp.zeros((64, HDIM), BF)
    wall[z, c, 0:SHARD_ROWS, :] = kw[...]
    wall[z, c, PAD_ROWS : PAD_ROWS + SHARD_ROWS, :] = vw[...]
    wall[z, c, 64:192, :] = qw[...]
    wall[z, c, 192:320, :] = ow[...]
    pl.semaphore_wait(barrier, len(peers) + 2 - jnp.where(self_half < 2, 1, 0))

    def gather1(a):
        return [push(a.at[x, y, 0], a.at[x, y, 0], at(dx=k)) for k in (1, 3, 2)] + [
            push(a.at[x, y, 1], a.at[x, y, 1], at(dy=k)) for k in (1, 3, 2)
        ]

    def gather2(a, first):
        for copy in first:
            copy.wait_recv()
        return [push(a.at[:, y, 0], a.at[:, y, 0], at(dy=k)) for k in (1, 3, 2)] + [
            push(a.at[x, :, 1], a.at[x, :, 1], at(dx=k)) for k in (1, 3, 2)
        ]

    def landed(copies):
        for copy in copies:
            copy.wait_recv()

    pieces = ((0, 192), (192, 128))
    limits = ((8, 7), (7, 8))
    arriving = {}

    def forward(j):
        for p, (start, rows) in enumerate(pieces):
            for side, sign in enumerate((1, -1)):
                block = wall.at[(z - sign * 2 * j + 16) % 16, c, pl.ds(start, rows)]
                for step in (2, 1):
                    if 2 * j + step <= limits[p][side]:
                        arriving[p, side, 2 * j + step] = push(block, block, at(dz=sign * step))

    def to_sibling(dz):
        block = wall.at[(z + dz + 16) % 16, c]
        return push(block, block, at(dc=1))

    def wait_blocks(k):
        for p in range(2):
            for side in range(2):
                if k <= limits[p][side]:
                    arriving[p, side, k].wait_recv()

    siblings = []
    forward(0)
    f1 = gather1(feats)
    g1 = gather1(gins)

    rows_iota = lax.broadcasted_iota(jnp.int32, (512, 512), 0)
    spread[...] = jnp.where(rows_iota == place[...], 1.0, 0.0).astype(BF)
    sorted_enc[...] = dot(spread[...], enc[...], 0, 0).astype(BF)

    def relay(source, target, base):
        for half in range(2):
            peer = low + 16 * half
            copy = pltpu.make_async_remote_copy(
                src_ref=source(half, peer),
                dst_ref=target,
                send_sem=send_sems.at[base + half],
                recv_sem=recv_sems.at[base + d // 16],
                device_id=(peer, m),
                device_id_type=MESH,
            )
            local = pltpu.make_async_copy(
                source(half, peer), target, recv_sems.at[base + d // 16]
            )

            @pl.when(self_half == half)
            def _():
                local.start()

            @pl.when(self_half != half)
            def _():
                copy.start()

    def relay_landed(source, target, base):
        for half in range(2):
            copy = pltpu.make_async_remote_copy(
                src_ref=source(half, low),
                dst_ref=target(half),
                send_sem=send_sems.at[base + half],
                recv_sem=recv_sems.at[base + half],
                device_id=(low + 16 * half, m),
                device_id_type=MESH,
            )
            copy.wait_recv()

            @pl.when(self_half != half)
            def _():
                copy.wait_send()

    base_a = count[0]
    count[0] += 2

    def slot_block(half, peer):
        return sorted_enc.at[pl.ds(pl.multiple_of(peer * 16, 16), 16), :]

    relay(slot_block, earr.at[x, y, d // 16], base_a)
    siblings.append(to_sibling(0))

    wait_blocks(2)
    forward(1)
    f2 = gather2(feats, f1)
    g2 = gather2(gins, g1)
    relay_landed(slot_block, lambda half: earr.at[x, y, half], base_a)
    e1 = gather1(earr)
    siblings += [to_sibling(2), to_sibling(-2)]
    wait_blocks(4)
    forward(2)
    wait_blocks(1)
    siblings += [to_sibling(1), to_sibling(-1)]
    e2 = gather2(earr, e1)
    siblings += [to_sibling(4), to_sibling(-4)]
    wait_blocks(6)
    forward(3)
    siblings += [to_sibling(6), to_sibling(-6)]
    wait_blocks(3)
    siblings += [to_sibling(3), to_sibling(-3)]

    order = omap[...]
    source = order >> 4
    rank = (((source + d) & 15) << 5) + ((source >> 4) << 4) + (order & 15)
    spread_o = jnp.where(rows_iota == rank, 1.0, 0.0).astype(BF)

    wait_blocks(5)
    siblings += [to_sibling(5), to_sibling(-5)]
    wait_blocks(7)
    siblings += [to_sibling(7), to_sibling(-7)]
    wait_blocks(8)
    siblings.append(to_sibling(8))
    landed(siblings)
    landed(e2)

    e_iota = lax.broadcasted_iota(jnp.int32, (ENC, 1024), 0)
    p_iota = lax.broadcasted_iota(jnp.int32, (ENC, 1024), 1)
    within = p_iota & 31
    select = jnp.where(
        (within < SHARD_ROWS) & ((p_iota >> 5) * SHARD_ROWS + within == e_iota), 1.0, 0.0
    ).astype(BF)
    padded = jnp.concatenate(
        [
            wall[:, :, 0:32, :].reshape(1024, HDIM),
            wall[:, :, 32:64, :].reshape(1024, HDIM),
        ],
        1,
    )
    kv_weight = dot(select, padded).astype(BF)
    arrived = earr[...].reshape(512, ENC)
    kv_arrived = dot(arrived, kv_weight).astype(BF)
    kvs[256:768, :] = dot(spread_o, kv_arrived, 0, 0).astype(BF)
    shift = push(kvs.at[pl.ds(512, 256)], kvs.at[pl.ds(0, 256)], after)

    landed(f2)
    landed(g2)

    def block_of(a, i):
        return a[i // 4, i % 4].reshape(128, 256)

    def wq(i):
        return wall[i, :, 64:192, :].reshape(256, HDIM)

    def wo(i):
        return jnp.concatenate([wall[i, 0, 192:320, :], wall[i, 1, 192:320, :]], 1)

    queries = jnp.zeros((128, HDIM), F32)
    d_att = jnp.zeros((128, HDIM), F32)
    for i in range(16):
        queries += dot(block_of(feats, i), wq(i))
        d_att += dot(block_of(gins, i), wo(i), 1, 1)
    queries = queries.astype(BF)
    d_att = d_att.astype(BF)

    shift.wait_recv()
    keys = kvs[:, 0:HDIM]
    values = kvs[:, HDIM:]
    token = lax.broadcasted_iota(jnp.int32, (128, 768), 0)
    column = lax.broadcasted_iota(jnp.int32, (128, 768), 1)
    stretch = jnp.where(token >= 63, 1, 0) + jnp.where(token >= 127, 1, 0)
    first = jnp.where(d % 16 == 0, 1, 0)
    mask = ((column >> 8) == stretch) & (stretch >= first)
    scores = jnp.where(mask, dot(queries, keys, 1, 1) * SCALE, -1e30)
    top = jnp.max(scores, -1, keepdims=True)
    expo = jnp.where(mask, jnp.exp(scores - top), 0.0)
    total = jnp.sum(expo, -1, keepdims=True)
    probs = expo / jnp.where(total > 0.0, total, 1.0)
    probs_half = probs.astype(BF)
    attended = dot(probs_half, values).astype(BF)
    grad_probs = dot(d_att, values, 1, 1)
    grad_scores = (
        probs * (grad_probs - jnp.sum(probs * grad_probs, -1, keepdims=True))
    ).astype(BF)
    key_terms = dot(grad_scores, queries, 0, 0) * SCALE
    value_terms = dot(probs_half, d_att, 0, 0)
    pair_terms = jnp.concatenate([key_terms, value_terms], 1)
    cbuf[...] = pair_terms[0:256].astype(BF)
    carry = push(cbuf, crecv, before)
    grad_queries = (dot(grad_scores, keys) * SCALE).astype(BF)

    def scatter1(a, land):
        return [
            push(a.at[(x + k) % 4, :, 0], land.at[0, k - 1], at(dx=k)) for k in (1, 3, 2)
        ] + [push(a.at[:, (y + k) % 4, 1], land.at[1, k - 1], at(dy=k)) for k in (1, 3, 2)]

    def add_up(parts):
        total = parts[0].astype(F32)
        for part in parts[1:]:
            total = total + part.astype(F32)
        return total.astype(BF)

    def scatter2(a, land, half_sum, land2, first):
        landed(first)
        half_sum[0] = add_up([a[x, :, 0]] + [land[0, k] for k in range(3)])
        half_sum[1] = add_up([a[:, y, 1]] + [land[1, k] for k in range(3)])
        return [
            push(half_sum.at[0, (y + k) % 4], land2.at[0, k - 1], at(dy=k)) for k in (1, 3, 2)
        ] + [
            push(half_sum.at[1, (x + k) % 4], land2.at[1, k - 1], at(dx=k)) for k in (1, 3, 2)
        ]

    def scattered(half_sum, land2, second):
        landed(second)
        return [
            add_up([half_sum[0, y]] + [land2[0, k] for k in range(3)]),
            add_up([half_sum[1, x]] + [land2[1, k] for k in range(3)]),
        ]

    def z_swap(t, s):
        return push(t.at[:, 1 - c], s, at(dc=1))

    def z_odd(t, s, u, odd, chain, swap, sign):
        swap.wait_recv()
        for k in range(16):
            there = (z + sign * k + 16) % 16
            u[(k % 2) * 8 + k // 2] = add_up([t[there, c], s[there]])
        return [
            push(u.at[pl.ds(8, 4)], odd.at[0], at(dz=sign)),
            push(u.at[pl.ds(12, 4)], odd.at[1], at(dz=-sign)),
            push(u.at[4], chain.at[0, 3], at(dz=2 * sign)),
        ]

    def z_chain(u, odd, chain, out, before_, sign, j):
        landed(before_)
        ahead = [u[j], odd[0, j]]
        if j < 4:
            ahead.append(chain[0, j])
        behind = [u[8 - j], odd[1, 3 - j]]
        if j < 3:
            behind.append(chain[1, j])
        out[0, j] = add_up(ahead)
        out[1, j] = add_up(behind)
        return [
            push(out.at[0, j], chain.at[0, j - 1], at(dz=2 * sign)),
            push(out.at[1, j], chain.at[1, j - 1], at(dz=-2 * sign)),
        ]

    def z_end(u, odd, chain, before_):
        landed(before_)
        return add_up([u[0], odd[0, 0], odd[1, 3], chain[0, 0], chain[1, 0]])

    for i in range(16):
        part = dot(attended, wo(i)).astype(BF)
        lp[i // 4, i % 4] = part.reshape(2, 64, 256)
    lp1 = scatter1(lp, rs1.at[0])
    for i in range(16):
        part = dot(attended, block_of(gins, i), 0, 0).astype(BF)
        tz[0, i, 0] = part[:, 0:HDIM]
        tz[0, i, 1] = part[:, HDIM:]
    out_swap = z_swap(tz.at[0], sib.at[0])
    carry.wait_recv()
    pair_own = jnp.concatenate(
        [pair_terms[256:512], pair_terms[512:768] + crecv[...].astype(F32)], 0
    ).astype(BF)
    pair_arr = dot(spread_o, pair_own).astype(BF)
    ep[...] = dot(pair_arr, kv_weight, 1, 1).astype(BF).reshape(4, 4, 2, 16, ENC)
    ep1 = scatter1(ep, rs1e)
    for i in range(16):
        part = dot(grad_queries, wq(i), 1, 1).astype(BF)
        ip[i // 4, i % 4] = part.reshape(2, 64, 256)
    ip1 = scatter1(ip, rs1.at[1])
    for i in range(16):
        part = dot(block_of(feats, i), grad_queries, 0, 0).astype(BF)
        tz[1, i] = part.reshape(2, 128, HDIM)
    query_swap = z_swap(tz.at[1], sib.at[1])
    pair_part = dot(arrived, pair_arr, 0, 0).astype(BF)
    tzk[...] = dot(select, pair_part, 0, 0).astype(BF).reshape(16, 2, 32, 256)
    pair_swap = z_swap(tzk, sibk)

    zs = [
        (uz.at[0], rodd.at[0], rch.at[0], chs.at[0], 1),
        (uz.at[1], rodd.at[1], rch.at[1], chs.at[1], -1),
        (uzk, roddk, rchk, chsk, 1),
    ]
    steps = [
        z_odd(tz.at[0], sib.at[0], uz.at[0], rodd.at[0], rch.at[0], out_swap, 1),
        z_odd(tz.at[1], sib.at[1], uz.at[1], rodd.at[1], rch.at[1], query_swap, -1),
        z_odd(tzk, sibk, uzk, roddk, rchk, pair_swap, 1),
    ]

    def z_all(j):
        for i, (u, odd, chain, out, sign) in enumerate(zs):
            steps[i] = z_chain(u, odd, chain, out, steps[i], sign, j)

    lp2 = scatter2(lp, rs1.at[0], mid.at[0], rs2.at[0], lp1)
    z_all(3)
    ep2 = scatter2(ep, rs1e, mide, rs2e, ep1)
    ip2 = scatter2(ip, rs1.at[1], mid.at[1], rs2.at[1], ip1)
    halves = scattered(mid.at[0], rs2.at[0], lp2)
    for h in range(2):
        layer_out[x, y, h] = halves[h]
    lo1 = gather1(layer_out)
    z_all(2)
    halves = scattered(mide, rs2e, ep2)
    for h in range(2):
        eout[h] = halves[h]
    base_b = count[0]
    count[0] += 2
    relay(lambda half, peer: eout.at[half], hall.at[x, y, d // 16], base_b)
    halves = scattered(mid.at[1], rs2.at[1], ip2)
    for h in range(2):
        input_grad[64 * h : 64 * h + 64, :] = halves[h]
    z_all(1)
    lo2 = gather2(layer_out, lo1)
    relay_landed(lambda half, peer: eout.at[half], lambda half: hall.at[x, y, half], base_b)
    h1 = gather1(hall)
    out_grad[...] = z_end(uz.at[0], rodd.at[0], rch.at[0], steps[0])
    query_grad[...] = z_end(uz.at[1], rodd.at[1], rch.at[1], steps[1])
    pair_grad[...] = z_end(uzk, roddk, rchk, steps[2])
    h2 = gather2(hall, h1)
    landed(lo2)
    landed(h2)
    for i in range(16):
        for half in range(2):
            owner = (i - d + 32) % 16 + 16 * half
            sorted_enc[pl.ds(pl.multiple_of(owner * 16, 16), 16), :] = hall[i // 4, i % 4, half]
    enc_grad[...] = dot(spread[...], sorted_enc[...]).astype(BF)
    for copy in sent:
        copy.wait_send()


def shards(
    tokens,
    encodings,
    shard_place,
    owner_map,
    query_weight,
    key_weight,
    value_weight,
    out_weight,
    grad_out,
):
    vmem = pl.BlockSpec(memory_space=pltpu.VMEM)
    outs = [
        jax.ShapeDtypeStruct((4, 4, 2, 64, 256), BF),
        jax.ShapeDtypeStruct((128, 256), BF),
        jax.ShapeDtypeStruct((128, 128), BF),
        jax.ShapeDtypeStruct((32, 256), BF),
        jax.ShapeDtypeStruct((128, 128), BF),
        jax.ShapeDtypeStruct((512, ENC), BF),
    ]
    shapes = [
        (4, 4, 2, 64, 256),
        (4, 4, 2, 64, 256),
        (16, 2, 320, 128),
        (512, 512),
        (512, ENC),
        (4, 4, 2, 16, ENC),
        (768, 256),
        (4, 4, 2, 64, 256),
        (4, 4, 2, 64, 256),
        (4, 4, 2, 16, ENC),
        (2, 2, 3, 4, 64, 256),
        (2, 3, 4, 16, ENC),
        (2, 2, 3, 64, 256),
        (2, 3, 16, ENC),
        (2, 2, 4, 64, 256),
        (2, 4, 16, ENC),
        (2, 16, 2, 128, 128),
        (16, 2, 32, 256),
        (2, 16, 128, 128),
        (16, 32, 256),
        (2, 16, 128, 128),
        (16, 32, 256),
        (2, 2, 4, 128, 128),
        (2, 4, 32, 256),
        (2, 2, 4, 128, 128),
        (2, 4, 32, 256),
        (2, 2, 4, 128, 128),
        (2, 4, 32, 256),
        (256, 256),
        (256, 256),
        (2, 16, ENC),
        (4, 4, 2, 16, ENC),
    ]
    scratch = [pltpu.VMEM(shape, BF) for shape in shapes]
    scratch += [
        pltpu.SemaphoreType.DMA((N_SEMS,)),
        pltpu.SemaphoreType.DMA((N_SEMS,)),
        pltpu.SemaphoreType.DMA((8,)),
    ]
    layer, input_grad, query_grad, pair_grad, out_grad, enc_grad = pl.pallas_call(
        kernel,
        out_shape=outs,
        in_specs=[vmem] * 9,
        out_specs=[vmem] * 6,
        scratch_shapes=scratch,
        compiler_params=pltpu.CompilerParams(
            collective_id=0, has_side_effects=True, vmem_limit_bytes=56 * 1024 * 1024
        ),
        name="retro",
    )(
        tokens,
        grad_out,
        query_weight,
        out_weight,
        key_weight,
        value_weight,
        encodings,
        shard_place,
        owner_map,
    )
    layer_out = layer.reshape(16, 128, 256).transpose(1, 0, 2).reshape(128, 4096)
    key_grad = pair_grad[:SHARD_ROWS, :HDIM]
    value_grad = pair_grad[:SHARD_ROWS, HDIM:]
    return (layer_out, input_grad, query_grad, key_grad, value_grad, out_grad, enc_grad)


def solution(mesh):
    placed = (
        P("dp", "mp"),
        P("dp", None),
        P("dp", None),
        P("dp", None),
        P("dp", "mp"),
        P("dp", "mp"),
        P("dp", "mp"),
        P("mp", "dp"),
        P("dp", "mp"),
    )
    return jax.shard_map(
        shards,
        mesh=mesh,
        in_specs=placed,
        out_specs=(
            P("dp", None),
            P("dp", "mp"),
            P("dp", "mp"),
            P("dp", "mp"),
            P("dp", "mp"),
            P("mp", "dp"),
            P("dp", None),
        ),
        check_vma=False,
    )
```

time: 752 us -> 112 us (0.15)
  waiting for transfers between devices: 464 us -> 0 us
  blocking collectives: 181 us -> 0 us
  Pallas kernels: 0 us -> 104 us
  starting transfers between devices: 50.4 us -> 0 us
  local copies, waits for them, and re-layouts: 25.1 us -> 6.07 us
  between operations: 15.3 us -> 0.67 us
  matrix products: 12.9 us -> 0 us
    all_gather x4 -> x0, waiting for transfers between devices: 149 us -> none  [the longest x1 73.9 us: shards(): query_full = lax.all_gather(query_weight, 'dp', axis=0, tiled=True)]
    psum x1 -> x0, waiting for transfers between devices: 110 us -> none  [shards(): layer_out = lax.psum(layer_part.astype(jnp.bfloat16), 'mp')]
    unnamed x14 -> x0, waiting for transfers between devices: 106 us -> none
    pallas_call x0 -> x1, Pallas kernels: none -> 104 us  [shards(): pl.pallas_call(kernel, out_shape=outs, in_specs=[vmem] * 9, out_specs=[vm...]
    all_gather x2 -> x0, blocking collectives: 94.9 us -> none  [the longest x1 66.6 us: shards(): lax.all_gather(key_weight, 'dp', axis=0, tiled=True)]
    reduce_scatter x1 -> x0, waiting for transfers between devices: 92 us -> none  [shards(): lax.psum_scatter(input_term.astype(jnp.bfloat16), 'mp', scatter_dimension...]
    unnamed x1 -> x0, blocking collectives: 85.8 us -> none
    all_to_all x2 -> x0, starting transfers between devices: 31.3 us -> none  [the longest x1 16.9 us: shards(): lax.all_to_all(outgoing, 'dp', split_axis=0, concat_axis=0, tiled=True)]
  transfers between devices with their start and end apart: 16 -> 0, of which waited for: 8 -> 0; matrix products, arithmetic and copies ran while one was open for 15% -> 0% of each run, Pallas kernels for 0% -> 0%
where the time goes in v1:
time: 112 us; the launch traced here: 111 us
  Pallas kernels  104 us (93%)
  local copies, waits for them, and re-layouts  6.07 us (5%)
    pallas_call x1, Pallas kernels, shards(): pl.pallas_call(kernel, out_shape=outs, in_specs=[vmem] * 9, out_specs=[vm...  104 us
    unnamed x14, local copies, waits for them, and re-layouts  3.08 us
    reshape x1, local copies, waits for them, and re-layouts, shards(): layer.reshape(16, 128, 256).transpose(1, 0, 2).reshape(128, 4096)  2.38 us

profile of v1, /device:TPU:1, one launch (start us, length us, event | category | flops | bytes accessed | tf_op | source)
XLA Modules:
  0.0 111.0 jit_solution(8456537293613513254)
XLA Ops:
  0.6 104.3 %retro.1 = (bf16[4,4,2,64,256]{4,3,2,1,0:T(8,128)(2,1)}, bf16[128,256]{1,0:T(8,128)(2,1)}, bf16[128,128]{1,0:T(8,128)(2,1)}, bf16[32,256]{1,0:T(8,128)(2,1)}, bf...) custom-call(bf16[128,256]{1,0:T(8,128)(2,1)} %tok.1, bf16[128,256]{1,0:T(8,128)(2,1)} %gout.1, bf16[128,128]{1,0:T(8,128)(2,1)} %qw.1, ...), custom_call_target="tpu_custom_call" | custom-call | tf_op jit(solution)/shard_map/retro/pallas_call | solution.py:520
  104.9 0.0 copy-start.4
  104.9 0.0 copy-start.1
  105.0 0.0 copy-start
  105.0 2.4 %copy.17 = bf16[16,16,8,256]{3,2,0,1:T(8,128)(2,1)} copy(bf16[16,16,8,256]{3,2,1,0:T(8,128)(2,1)} %bitcast.6) | data formatting | bytes 2097152 | tf_op jit(solution)/shard_map/reshape | solution.py:541
  107.3 0.0 copy-done.4
  107.3 0.6 fusion
  108.0 0.0 copy-done.1
  108.0 0.0 copy-start.3
  108.0 0.6 copy.22
  108.6 0.1 copy-done.3
  108.7 0.0 copy-start.2
  108.7 0.6 copy.23
  109.3 0.2 copy-done.2
  109.5 0.6 copy.24
  110.1 0.0 copy-done
  110.1 0.9 copy.25
Async XLA Ops:
  104.9 2.4 %copy-start.4 = (bf16[32,256]{1,0:T(8,128)(2,1)S(1)}, bf16[32,256]{1,0:T(8,128)(2,1)}, u32[]{:S(2)}) copy-start(bf16[32,256]{1,0:T(8,128)(2,1)} %get-tuple-element.16) | copy-start | bytes 49156
  104.9 3.0 %copy-start.1 = (bf16[128,256]{1,0:T(8,128)(2,1)S(1)}, bf16[128,256]{1,0:T(8,128)(2,1)}, u32[]{:S(2)}) copy-start(bf16[128,256]{1,0:T(8,128)(2,1)} %get-tuple-element.29) | copy-start | bytes 196612
  105.0 5.2 %copy-start = (bf16[512,896]{1,0:T(8,128)(2,1)S(1)}, bf16[512,896]{1,0:T(8,128)(2,1)}, u32[]{:S(2)}) copy-start(bf16[512,896]{1,0:T(8,128)(2,1)} %get-tuple-element.34) | copy-start | bytes 2752516
  108.0 0.8 copy-start.3
  108.7 0.8 copy-start.2

commit v2 on v1

v2 whole, which is shorter than its diff:
```python
import jax
import jax.numpy as jnp
from jax import lax
from jax.experimental import pallas as pl
from jax.experimental.pallas import tpu as pltpu
from jax.sharding import PartitionSpec as P

HDIM = 128
ENC = 896
SHARD_ROWS = 28
PAD_ROWS = 32
SCALE = HDIM ** (-0.5)
BF = jnp.bfloat16
F32 = jnp.float32
N_SEMS = 113
MESH = pl.DeviceIdType.MESH


def dot(a, b, ca=1, cb=0):
    return lax.dot_general(a, b, (((ca,), (cb,)), ((), ())), preferred_element_type=F32)


def kernel(
    tok,
    gout,
    qw,
    ow,
    kw,
    vw,
    enc,
    place,
    omap,
    layer_hbm,
    input_hbm,
    query_hbm,
    pair_hbm,
    out_hbm,
    enc_hbm,
    encs,
    flat,
    layer_out,
    input_grad,
    query_grad,
    pair_grad,
    out_grad,
    enc_grad,
    feats,
    gins,
    wall,
    spread,
    sorted_enc,
    relayed,
    earr,
    kvs,
    lp,
    ip,
    ep,
    rs1,
    rs1e,
    rs2,
    rs2e,
    mid,
    mide,
    tz,
    tzk,
    sib,
    sibk,
    uz,
    uzk,
    rodd,
    roddk,
    rch,
    rchk,
    chs,
    chsk,
    cbuf,
    crecv,
    eout,
    hall,
    many,
    many_e,
    sems,
    local_sems,
):
    d = lax.axis_index("dp")
    m = lax.axis_index("mp")
    z, c = d // 2, d % 2
    x, y = m // 4, m % 4

    def at(dz=0, dc=0, dx=0, dy=0):
        return (((z + dz + 16) % 16) * 2 + (c + dc) % 2, ((x + dx) % 4) * 4 + (y + dy) % 4)

    count = [0]
    finals = []

    def sem():
        count[0] += 1
        return sems.at[count[0] - 1]

    def push(src, dst, to, send, recv):
        pltpu.make_async_remote_copy(
            src_ref=src,
            dst_ref=dst,
            send_sem=send,
            recv_sem=recv,
            device_id=to,
            device_id_type=MESH,
        ).start()

    def drain(ref, one):
        pltpu.make_async_copy(ref, ref, one).wait()

    low = (m - d + 32) % 16
    self_half = jnp.where(low == d % 16, d // 16, 2)

    barrier = pltpu.get_barrier_semaphore()
    after = ((d + 1) % 32, m)
    before = ((d + 31) % 32, m)
    peers = [at(dx=k) for k in (1, 2, 3)] + [at(dy=k) for k in (1, 2, 3)]
    peers += [at(dz=k) for k in (1, -1, 2, -2)] + [at(dc=1), after, before]
    for peer in peers:
        pl.semaphore_signal(barrier, inc=1, device_id=peer, device_id_type=MESH)
    for half in range(2):
        @pl.when(self_half != half)
        def _():
            pl.semaphore_signal(barrier, inc=1, device_id=(low + 16 * half, m), device_id_type=MESH)

    loads = [
        (enc, encs),
        (qw, wall.at[z, c, pl.ds(64, 128)]),
        (ow, wall.at[z, c, pl.ds(192, 128)]),
    ]
    for h in range(2):
        loads.append((tok.at[pl.ds(64 * h, 64)], feats.at[x, y, h]))
        loads.append((gout.at[pl.ds(64 * h, 64)], gins.at[x, y, h]))
    loads = [
        pltpu.make_async_copy(src, dst, local_sems.at[i]) for i, (src, dst) in enumerate(loads)
    ]
    for load in loads:
        load.start()
    wall[z, c, 0:64, :] = jnp.zeros((64, HDIM), BF)
    wall[z, c, 0:SHARD_ROWS, :] = kw[...]
    wall[z, c, PAD_ROWS : PAD_ROWS + SHARD_ROWS, :] = vw[...]

    rows_iota = lax.broadcasted_iota(jnp.int32, (512, 512), 0)
    spread[...] = jnp.where(rows_iota == place[...], 1.0, 0.0).astype(BF)
    loads[0].wait()
    r_iota = lax.broadcasted_iota(jnp.int32, (32, 512), 0)
    s_iota = lax.broadcasted_iota(jnp.int32, (32, 512), 1)
    picked = low * 16 + r_iota + jnp.where(r_iota >= 16, 240, 0)
    pick = jnp.where(s_iota == picked, 1.0, 0.0).astype(BF)
    chosen = dot(pick, spread[...], 1, 1).astype(BF)
    relayed[...] = dot(chosen, encs[...]).astype(BF).reshape(2, 16, ENC)
    for load in loads[1:]:
        load.wait()
    stores = []

    def store(src, dst):
        copy = pltpu.make_async_copy(src, dst, local_sems.at[8 + len(stores)])
        copy.start()
        stores.append(copy)

    pl.semaphore_wait(barrier, len(peers) + 2 - jnp.where(self_half < 2, 1, 0))

    def gather1(a, wide):
        send, rest = sem(), sem()
        finals.append((wide, send))
        ahead = [sem() for _ in range(3)]
        across = [sem() for _ in range(3)]
        block0, block1 = a.at[x, y, 0], a.at[x, y, 1]
        for i, k in enumerate((1, 3, 2)):
            push(block0, block0, at(dx=k), send, ahead[i])
            push(block1, block1, at(dy=k), send, across[i])
        for k in (1, 3, 2):
            push(block0, block0, at(dy=k), send, rest)
            push(block1, block1, at(dx=k), send, rest)
        return send, rest, ahead, across

    def gather2(a, first):
        send, rest, ahead, across = first
        for i, k in enumerate((1, 3, 2)):
            block = a.at[(x + 4 - k) % 4, y, 0]
            drain(block, ahead[i])
            for j in (1, 3, 2):
                push(block, block, at(dy=j), send, rest)
            block = a.at[x, (y + 4 - k) % 4, 1]
            drain(block, across[i])
            for j in (1, 3, 2):
                push(block, block, at(dx=j), send, rest)
        return a.at[pl.ds(0, 3)], rest

    def landed(end):
        drain(*end)

    pieces = ((0, 64), (64, 128), (192, 128))
    limits = ((8, 7), (7, 8), (8, 7))
    arriving = [{k: sem() for k in range(1, 9)} for _ in pieces]
    sending = [sem() for _ in pieces]
    for (start, rows), one in zip(pieces, sending):
        finals.append((wall.at[pl.ds(0, 15), 0, pl.ds(start, rows)], one))

    def forward(p, j):
        start, rows = pieces[p]
        for step in (2, 1):
            k = 2 * j + step
            for side, sign in enumerate((1, -1)):
                if k <= limits[p][side]:
                    block = wall.at[(z - sign * 2 * j + 16) % 16, c, pl.ds(start, rows)]
                    push(block, block, at(dz=sign * step), sending[p], arriving[p][k])

    crossing = {0: (sem(), sem()), 64: (sem(), sem())}
    for start, rows in ((0, 64), (64, 256)):
        finals.append((wall.at[:, 0, pl.ds(start, rows)], crossing[start][0]))

    def to_sibling(dz, start, rows):
        block = wall.at[(z + dz + 16) % 16, c, pl.ds(start, rows)]
        push(block, block, at(dc=1), *crossing[start])

    def all_crossed(start, rows):
        drain(wall.at[:, 0, pl.ds(start, rows)], crossing[start][1])

    def wait_blocks(p, k):
        start, rows = pieces[p]
        drain(wall.at[pl.ds(0, len(both(k))), 0, pl.ds(start, rows)], arriving[p][k])

    def both(k):
        return (k, -k) if k < 8 else (8,)

    def relay(source, target, pair):
        sends, recvs = pair
        for half in range(2):
            peer = low + 16 * half

            @pl.when(self_half == half)
            def _():
                pltpu.make_async_copy(source.at[half], target, recvs.at[d // 16]).start()

            @pl.when(self_half != half)
            def _():
                push(source.at[half], target, (peer, m), sends.at[half], recvs.at[d // 16])

    def relay_landed(source, target, pair):
        sends, recvs = pair
        for half in range(2):
            drain(target(half), recvs.at[half])

            @pl.when(self_half != half)
            def _():
                drain(source.at[half], sends.at[half])

    def two():
        count[0] += 2
        return sems.at[pl.ds(count[0] - 2, 2)]

    pair_a = two(), two()
    relay(relayed, earr.at[x, y, d // 16], pair_a)
    forward(0, 0)
    f1 = gather1(feats, many)
    forward(1, 0)
    g1 = gather1(gins, many)
    forward(2, 0)
    to_sibling(0, 0, 64)
    to_sibling(0, 64, 256)
    order = omap[...]
    source = order >> 4
    rank = (((source + d) & 15) << 5) + ((source >> 4) << 4) + (order & 15)
    spread_o = jnp.where(rows_iota == rank, 1.0, 0.0).astype(BF)

    e_iota = lax.broadcasted_iota(jnp.int32, (ENC, 1024), 0)
    p_iota = lax.broadcasted_iota(jnp.int32, (ENC, 1024), 1)
    within = p_iota & 31
    select = jnp.where(
        (within < SHARD_ROWS) & ((p_iota >> 5) * SHARD_ROWS + within == e_iota), 1.0, 0.0
    ).astype(BF)

    for p in range(3):
        wait_blocks(p, 2)
        forward(p, 1)
    relay_landed(relayed, lambda half: earr.at[x, y, half], pair_a)
    e1 = gather1(earr, many_e)
    for i in both(2):
        to_sibling(i, 0, 64)
    for i in both(2):
        to_sibling(i, 64, 256)
    f2 = gather2(feats, f1)
    for p in range(3):
        wait_blocks(p, 4)
        forward(p, 2)
    e2 = gather2(earr, e1)
    g2 = gather2(gins, g1)
    for i in both(4):
        to_sibling(i, 0, 64)
    for i in both(4):
        to_sibling(i, 64, 256)
    for k in (1, 3):
        wait_blocks(0, k)
        for i in both(k):
            to_sibling(i, 0, 64)
    for p in range(3):
        wait_blocks(p, 6)
        forward(p, 3)
    for i in both(6):
        to_sibling(i, 0, 64)
    for i in both(6):
        to_sibling(i, 64, 256)
    for k in (1, 3):
        wait_blocks(1, k)
        wait_blocks(2, k)
        for i in both(k):
            to_sibling(i, 64, 256)
    for k in (5, 7, 8):
        wait_blocks(0, k)
        for i in both(k):
            to_sibling(i, 0, 64)
    all_crossed(0, 64)
    landed(e2)

    padded = jnp.concatenate(
        [
            wall[:, :, 0:32, :].reshape(1024, HDIM),
            wall[:, :, 32:64, :].reshape(1024, HDIM),
        ],
        1,
    )
    kv_weight = dot(select, padded).astype(BF)
    arrived = earr[...].reshape(512, ENC)
    kv_arrived = dot(arrived, kv_weight).astype(BF)
    kvs[256:768, :] = dot(spread_o, kv_arrived, 0, 0).astype(BF)
    shift = sem(), sem()
    finals.append((kvs.at[pl.ds(0, 256)], shift[0]))
    push(kvs.at[pl.ds(512, 256)], kvs.at[pl.ds(0, 256)], after, *shift)

    landed(f2)
    landed(g2)

    def block_of(a, i):
        return a[i // 4, i % 4].reshape(128, 256)

    def wq(i):
        return wall[i, :, 64:192, :].reshape(256, HDIM)

    def wo(i):
        return jnp.concatenate([wall[i, 0, 192:320, :], wall[i, 1, 192:320, :]], 1)

    queries = jnp.zeros((128, HDIM), F32)
    d_att = jnp.zeros((128, HDIM), F32)
    for k in (0, 2, 4, 6, 1, 3, 5, 7, 8):
        if k in (5, 7, 8):
            wait_blocks(1, k)
            wait_blocks(2, k)
            for i in both(k):
                to_sibling(i, 64, 256)
    all_crossed(64, 256)
    for k in (0, 2, 4, 6, 1, 3, 5, 7, 8):
        for dz in (0,) if k == 0 else both(k):
            i = (z + dz + 16) % 16
            queries += dot(block_of(feats, i), wq(i))
            d_att += dot(block_of(gins, i), wo(i), 1, 1)
    queries = queries.astype(BF)
    d_att = d_att.astype(BF)

    drain(kvs.at[pl.ds(0, 256)], shift[1])
    keys = kvs[:, 0:HDIM]
    values = kvs[:, HDIM:]
    token = lax.broadcasted_iota(jnp.int32, (128, 768), 0)
    column = lax.broadcasted_iota(jnp.int32, (128, 768), 1)
    stretch = jnp.where(token >= 63, 1, 0) + jnp.where(token >= 127, 1, 0)
    first = jnp.where(d % 16 == 0, 1, 0)
    mask = ((column >> 8) == stretch) & (stretch >= first)
    scores = jnp.where(mask, dot(queries, keys, 1, 1) * SCALE, -1e30)
    top = jnp.max(scores, -1, keepdims=True)
    expo = jnp.where(mask, jnp.exp(scores - top), 0.0)
    total = jnp.sum(expo, -1, keepdims=True)
    probs = expo / jnp.where(total > 0.0, total, 1.0)
    probs_half = probs.astype(BF)
    attended = dot(probs_half, values).astype(BF)
    grad_probs = dot(d_att, values, 1, 1)
    grad_scores = (
        probs * (grad_probs - jnp.sum(probs * grad_probs, -1, keepdims=True))
    ).astype(BF)
    key_terms = dot(grad_scores, queries, 0, 0) * SCALE
    value_terms = dot(probs_half, d_att, 0, 0)
    pair_terms = jnp.concatenate([key_terms, value_terms], 1)
    cbuf[...] = pair_terms[0:256].astype(BF)
    carry = sem(), sem()
    finals.append((cbuf, carry[0]))
    push(cbuf, crecv, before, *carry)
    grad_queries = (dot(grad_scores, keys) * SCALE).astype(BF)

    def scatter1(a, land, wide):
        send, recv = sem(), sem()
        finals.append((wide, send))
        for k in (1, 3, 2):
            push(a.at[(x + k) % 4, :, 0], land.at[0, k - 1], at(dx=k), send, recv)
            push(a.at[:, (y + k) % 4, 1], land.at[1, k - 1], at(dy=k), send, recv)
        return send, recv

    def add_up(parts):
        total = parts[0].astype(F32)
        for part in parts[1:]:
            total = total + part.astype(F32)
        return total.astype(BF)

    def scatter2(a, land, half_sum, land2, first):
        send, recv = first
        drain(land, recv)
        half_sum[0] = add_up([a[x, :, 0]] + [land[0, k] for k in range(3)])
        half_sum[1] = add_up([a[:, y, 1]] + [land[1, k] for k in range(3)])
        recv = sem()
        for k in (1, 3, 2):
            push(half_sum.at[0, (y + k) % 4], land2.at[0, k - 1], at(dy=k), send, recv)
            push(half_sum.at[1, (x + k) % 4], land2.at[1, k - 1], at(dx=k), send, recv)
        return recv

    def scattered(half_sum, land2, recv):
        drain(land2, recv)
        return [
            add_up([half_sum[0, y]] + [land2[0, k] for k in range(3)]),
            add_up([half_sum[1, x]] + [land2[1, k] for k in range(3)]),
        ]

    def z_swap(t, s):
        send, recv = sem(), sem()
        finals.append((s, send))
        push(t.at[:, 1 - c], s, at(dc=1), send, recv)
        return recv

    def z_odd(t, s, u, odd, chain, swap, sign):
        drain(s, swap)
        for k in range(16):
            there = (z + sign * k + 16) % 16
            u[(k % 2) * 8 + k // 2] = add_up([t[there, c], s[there]])
        send, recv = sem(), sem()
        finals.append((u.at[pl.ds(0, 15)], send))
        push(u.at[4], chain.at[0, 3], at(dz=2 * sign), send, recv)
        push(u.at[pl.ds(8, 4)], odd.at[0], at(dz=sign), send, recv)
        push(u.at[pl.ds(12, 4)], odd.at[1], at(dz=-sign), send, recv)
        return send, recv, u.at[pl.ds(0, 9)]

    def z_chain(u, odd, chain, out, step, sign, j):
        send, recv, size = step
        drain(size, recv)
        ahead = [u[j], odd[0, j], chain[0, j]]
        behind = [u[8 - j], odd[1, 3 - j]]
        if j < 3:
            behind.append(chain[1, j])
        out[0, j] = add_up(ahead)
        out[1, j] = add_up(behind)
        recv = sem()
        push(out.at[0, j], chain.at[0, j - 1], at(dz=2 * sign), send, recv)
        push(out.at[1, j], chain.at[1, j - 1], at(dz=-2 * sign), send, recv)
        return send, recv, u.at[pl.ds(0, 2)]

    def z_end(u, odd, chain, step):
        drain(step[2], step[1])
        return add_up([u[0], odd[0, 0], odd[1, 3], chain[0, 0], chain[1, 0]])

    for i in range(16):
        part = dot(attended, wo(i)).astype(BF)
        lp[i // 4, i % 4] = part.reshape(2, 64, 256)
    lp1 = scatter1(lp, rs1.at[0], many)
    for i in range(16):
        part = dot(attended, block_of(gins, i), 0, 0).astype(BF)
        tz[0, i, 0] = part[:, 0:HDIM]
        tz[0, i, 1] = part[:, HDIM:]
    out_swap = z_swap(tz.at[0], sib.at[0])
    drain(crecv, carry[1])
    pair_own = jnp.concatenate(
        [pair_terms[256:512], pair_terms[512:768] + crecv[...].astype(F32)], 0
    ).astype(BF)
    pair_arr = dot(spread_o, pair_own).astype(BF)
    ep[...] = dot(pair_arr, kv_weight, 1, 1).astype(BF).reshape(4, 4, 2, 16, ENC)
    ep1 = scatter1(ep, rs1e, many_e)
    for i in range(16):
        part = dot(grad_queries, wq(i), 1, 1).astype(BF)
        ip[i // 4, i % 4] = part.reshape(2, 64, 256)
    ip1 = scatter1(ip, rs1.at[1], many)
    for i in range(16):
        part = dot(block_of(feats, i), grad_queries, 0, 0).astype(BF)
        tz[1, i] = part.reshape(2, 128, HDIM)
    query_swap = z_swap(tz.at[1], sib.at[1])
    pair_part = dot(arrived, pair_arr, 0, 0).astype(BF)
    tzk[...] = dot(select, pair_part, 0, 0).astype(BF).reshape(16, 2, 32, 256)
    pair_swap = z_swap(tzk, sibk)

    zs = [
        (uz.at[0], rodd.at[0], rch.at[0], chs.at[0], 1),
        (uz.at[1], rodd.at[1], rch.at[1], chs.at[1], -1),
        (uzk, roddk, rchk, chsk, 1),
    ]
    steps = [
        z_odd(tz.at[0], sib.at[0], uz.at[0], rodd.at[0], rch.at[0], out_swap, 1),
        z_odd(tz.at[1], sib.at[1], uz.at[1], rodd.at[1], rch.at[1], query_swap, -1),
        z_odd(tzk, sibk, uzk, roddk, rchk, pair_swap, 1),
    ]

    def z_all(j):
        for i, (u, odd, chain, out, sign) in enumerate(zs):
            steps[i] = z_chain(u, odd, chain, out, steps[i], sign, j)

    lp2 = scatter2(lp, rs1.at[0], mid.at[0], rs2.at[0], lp1)
    ep2 = scatter2(ep, rs1e, mide, rs2e, ep1)
    z_all(3)
    halves = scattered(mid.at[0], rs2.at[0], lp2)
    for h in range(2):
        layer_out[x, y, h] = halves[h]
    lo1 = gather1(layer_out, many)
    halves = scattered(mide, rs2e, ep2)
    for h in range(2):
        eout[h] = halves[h]
    pair_b = two(), two()
    relay(eout, hall.at[x, y, d // 16], pair_b)
    ip2 = scatter2(ip, rs1.at[1], mid.at[1], rs2.at[1], ip1)
    z_all(2)
    lo2 = gather2(layer_out, lo1)
    relay_landed(eout, lambda half: hall.at[x, y, half], pair_b)
    h1 = gather1(hall, many_e)
    z_all(1)
    halves = scattered(mid.at[1], rs2.at[1], ip2)
    for h in range(2):
        input_grad[64 * h : 64 * h + 64, :] = halves[h]
    store(input_grad, input_hbm)
    h2 = gather2(hall, h1)
    out_grad[...] = z_end(uz.at[0], rodd.at[0], rch.at[0], steps[0])
    store(out_grad, out_hbm)
    query_grad[...] = z_end(uz.at[1], rodd.at[1], rch.at[1], steps[1])
    store(query_grad, query_hbm)
    pair_grad[...] = z_end(uzk, roddk, rchk, steps[2])
    store(pair_grad, pair_hbm)
    landed(lo2)
    for i in range(16):
        flat[:, 256 * i : 256 * i + 256] = block_of(layer_out, i)
    store(flat, layer_hbm)
    landed(h2)
    for i in range(16):
        for half in range(2):
            owner = (i - d + 32) % 16 + 16 * half
            sorted_enc[pl.ds(pl.multiple_of(owner * 16, 16), 16), :] = hall[i // 4, i % 4, half]
    enc_grad[...] = dot(spread[...], sorted_enc[...]).astype(BF)
    store(enc_grad, enc_hbm)
    for copy in stores:
        copy.wait()
    for end in finals:
        drain(*end)
    assert count[0] == N_SEMS, count[0]


def finish(
    layer, input_g, query_g, pair_g, out_g, enc_g,
    layer_out, input_out, query_out, key_out, value_out, out_out, enc_out,
    held_l, held_i, held_q, held_p, held_o, held_e, sems,
):
    pairs = [
        (layer, held_l, layer_out),
        (enc_g, held_e, enc_out),
        (input_g, held_i, input_out),
        (query_g, held_q, query_out),
        (out_g, held_o, out_out),
    ]
    ins = [
        pltpu.make_async_copy(src, held, sems.at[i]) for i, (src, held, _) in enumerate(pairs)
    ]
    outs = [
        pltpu.make_async_copy(held, dst, sems.at[8 + i])
        for i, (_, held, dst) in enumerate(pairs)
    ]
    pair_in = pltpu.make_async_copy(pair_g, held_p, sems.at[7])
    pair_in.start()
    for copy in ins:
        copy.start()
    pair_in.wait()
    key_out[...] = held_p[0:SHARD_ROWS, 0:HDIM]
    value_out[...] = held_p[0:SHARD_ROWS, HDIM:]
    for copy, onward in zip(ins, outs):
        copy.wait()
        onward.start()
    for copy in outs:
        copy.wait()


def shards(
    tokens,
    encodings,
    shard_place,
    owner_map,
    query_weight,
    key_weight,
    value_weight,
    out_weight,
    grad_out,
):
    vmem = pl.BlockSpec(memory_space=pltpu.VMEM)
    hbm = pl.BlockSpec(memory_space=pl.ANY)
    outs = [
        jax.ShapeDtypeStruct((128, 4096), BF),
        jax.ShapeDtypeStruct((128, 256), BF),
        jax.ShapeDtypeStruct((128, 128), BF),
        jax.ShapeDtypeStruct((32, 256), BF),
        jax.ShapeDtypeStruct((128, 128), BF),
        jax.ShapeDtypeStruct((512, ENC), BF),
    ]
    shapes = [
        (512, ENC),
        (128, 4096),
        (4, 4, 2, 64, 256),
        (128, 256),
        (128, 128),
        (32, 256),
        (128, 128),
        (512, ENC),
        (4, 4, 2, 64, 256),
        (4, 4, 2, 64, 256),
        (16, 2, 320, 128),
        (512, 512),
        (512, ENC),
        (2, 16, ENC),
        (4, 4, 2, 16, ENC),
        (768, 256),
        (4, 4, 2, 64, 256),
        (4, 4, 2, 64, 256),
        (4, 4, 2, 16, ENC),
        (2, 2, 3, 4, 64, 256),
        (2, 3, 4, 16, ENC),
        (2, 2, 3, 64, 256),
        (2, 3, 16, ENC),
        (2, 2, 4, 64, 256),
        (2, 4, 16, ENC),
        (2, 16, 2, 128, 128),
        (16, 2, 32, 256),
        (2, 16, 128, 128),
        (16, 32, 256),
        (2, 16, 128, 128),
        (16, 32, 256),
        (2, 2, 4, 128, 128),
        (2, 4, 32, 256),
        (2, 2, 4, 128, 128),
        (2, 4, 32, 256),
        (2, 2, 4, 128, 128),
        (2, 4, 32, 256),
        (256, 256),
        (256, 256),
        (2, 16, ENC),
        (4, 4, 2, 16, ENC),
        (30, 64, 256),
        (30, 16, ENC),
    ]
    scratch = [pltpu.VMEM(shape, BF) for shape in shapes]
    scratch += [
        pltpu.SemaphoreType.DMA((N_SEMS,)),
        pltpu.SemaphoreType.DMA((14,)),
    ]
    parts = pl.pallas_call(
        kernel,
        out_shape=outs,
        in_specs=[hbm] * 4 + [vmem] * 2 + [hbm] + [vmem] * 2,
        out_specs=[hbm] * 6,
        scratch_shapes=scratch,
        compiler_params=pltpu.CompilerParams(
            collective_id=0, has_side_effects=True, vmem_limit_bytes=56 * 1024 * 1024
        ),
        name="retro",
    )(
        tokens,
        grad_out,
        query_weight,
        out_weight,
        key_weight,
        value_weight,
        encodings,
        shard_place,
        owner_map,
    )
    shapes = [
        (128, 4096),
        (128, 256),
        (128, 128),
        (SHARD_ROWS, 128),
        (SHARD_ROWS, 128),
        (128, 128),
        (512, ENC),
    ]
    return pl.pallas_call(
        finish,
        out_shape=[jax.ShapeDtypeStruct(shape, BF) for shape in shapes],
        in_specs=[hbm] * 6,
        out_specs=[hbm] * 3 + [vmem] * 2 + [hbm] * 2,
        scratch_shapes=[
            pltpu.VMEM((128, 4096), BF),
            pltpu.VMEM((128, 256), BF),
            pltpu.VMEM((128, 128), BF),
            pltpu.VMEM((32, 256), BF),
            pltpu.VMEM((128, 128), BF),
            pltpu.VMEM((512, ENC), BF),
            pltpu.SemaphoreType.DMA((16,)),
        ],
        name="finish",
    )(*parts)


def solution(mesh):
    placed = (
        P("dp", "mp"),
        P("dp", None),
        P("dp", None),
        P("dp", None),
        P("dp", "mp"),
        P("dp", "mp"),
        P("dp", "mp"),
        P("mp", "dp"),
        P("dp", "mp"),
    )
    return jax.shard_map(
        shards,
        mesh=mesh,
        in_specs=placed,
        out_specs=(
            P("dp", None),
            P("dp", "mp"),
            P("dp", "mp"),
            P("dp", "mp"),
            P("dp", "mp"),
            P("mp", "dp"),
            P("dp", None),
        ),
        check_vma=False,
    )
```

time: 112 us -> 93.7 us (0.84)
  Pallas kernels: 104 us -> 92.8 us
  local copies, waits for them, and re-layouts: 6.07 us -> 0 us
    pallas_call x1 -> x2, Pallas kernels: 104 us -> 92.8 us  [the longest x1 89.5 us: shards(): pl.pallas_call(kernel, out_shape=outs, in_specs=[hbm] * 4 + [vmem] * 2 +...]
    unnamed x14 -> x0, local copies, waits for them, and re-layouts: 3.08 us -> none
    reshape x1 -> x0, local copies, waits for them, and re-layouts: 2.38 us -> none  [shards(): layer.reshape(16, 128, 256).transpose(1, 0, 2).reshape(128, 4096)]
where the time goes in v2:
time: 93.7 us; the launch traced here: 93.4 us
  Pallas kernels  92.8 us (99%)
    pallas_call x1, Pallas kernels, shards(): pl.pallas_call(kernel, out_shape=outs, in_specs=[hbm] * 4 + [vmem] * 2 +...  89.5 us
    pallas_call x1, Pallas kernels, shards(): pl.pallas_call(finish, out_shape=[jax.ShapeDtypeStruct(shape, BF) for sha...  3.28 us

profile of v2, /device:TPU:1, one launch (start us, length us, event | category | flops | bytes accessed | tf_op | source)
XLA Modules:
  0.0 93.4 jit_solution(745067673061108664)
XLA Ops:
  0.6 89.5 %retro.1 = (bf16[128,4096]{1,0:T(8,128)(2,1)}, bf16[128,256]{1,0:T(8,128)(2,1)}, bf16[128,128]{1,0:T(8,128)(2,1)}, bf16[32,256]{1,0:T(8,128)(2,1)}, bf16[128,128]{1,0:T(8,128)(2,1)}, /*index=5*/bf16[512,896]{1,0:T(8,128)(2,1)}) custom-call(bf16[128,256]{1,0:T(8,128)(2,1)} %tok.1, bf16[128,256]{1,0:T(8,128)(2,1)} %gout.1, bf16[128,128]{1,0:T(8,128)(2,1)} %qw.1, ...), custom_call_target="tpu_custom_call" | custom-call | tf_op jit(solution)/shard_map/retro/pallas_call | solution.py:652
  90.1 3.3 %finish.1 = (bf16[128,4096]{1,0:T(8,128)(2,1)}, bf16[128,256]{1,0:T(8,128)(2,1)}, bf16[128,128]{1,0:T(8,128)(2,1)}, bf16[28,128]{1,0:T(8,128)(2,1)}, bf16[28,128...) custom-call(bf16[128,4096]{1,0:T(8,128)(2,1)} %get-tuple-element.13.layer, ...), custom_call_target="tpu_custom_call" | custom-call | tf_op jit(solution)/shard_map/finish/pallas_call | solution.py:682

commit v3 on v2

--- a/solution.py
+++ b/solution.py
@@ -12,7 +12,7 @@
 SCALE = HDIM ** (-0.5)
 BF = jnp.bfloat16
 F32 = jnp.float32
-N_SEMS = 113
+N_SEMS = 115
 MESH = pl.DeviceIdType.MESH
 
 
@@ -194,6 +194,7 @@
 
     pieces = ((0, 64), (64, 128), (192, 128))
     limits = ((8, 7), (7, 8), (8, 7))
+    strides = (2, 2, 2)
     arriving = [{k: sem() for k in range(1, 9)} for _ in pieces]
     sending = [sem() for _ in pieces]
     for (start, rows), one in zip(pieces, sending):
@@ -201,30 +202,46 @@
 
     def forward(p, j):
         start, rows = pieces[p]
-        for step in (2, 1):
-            k = 2 * j + step
+        base = strides[p] * j
+        for step in range(strides[p], 0, -1):
+            k = base + step
             for side, sign in enumerate((1, -1)):
                 if k <= limits[p][side]:
-                    block = wall.at[(z - sign * 2 * j + 16) % 16, c, pl.ds(start, rows)]
+                    block = wall.at[(z - sign * base + 16) % 16, c, pl.ds(start, rows)]
                     push(block, block, at(dz=sign * step), sending[p], arriving[p][k])
 
-    crossing = {0: (sem(), sem()), 64: (sem(), sem())}
-    for start, rows in ((0, 64), (64, 256)):
-        finals.append((wall.at[:, 0, pl.ds(start, rows)], crossing[start][0]))
-
-    def to_sibling(dz, start, rows):
-        block = wall.at[(z + dz + 16) % 16, c, pl.ds(start, rows)]
-        push(block, block, at(dc=1), *crossing[start])
-
-    def all_crossed(start, rows):
-        drain(wall.at[:, 0, pl.ds(start, rows)], crossing[start][1])
-
-    def wait_blocks(p, k):
+    crossing = [(sem(), sem()) for _ in pieces]
+    for (start, rows), one in zip(pieces, crossing):
+        finals.append((wall.at[:, 0, pl.ds(start, rows)], one[0]))
+
+    def to_sibling(p, *ks):
         start, rows = pieces[p]
-        drain(wall.at[pl.ds(0, len(both(k))), 0, pl.ds(start, rows)], arriving[p][k])
+        for k in ks:
+            for dz in both(k):
+                block = wall.at[(z + dz + 16) % 16, c, pl.ds(start, rows)]
+                push(block, block, at(dc=1), *crossing[p])
+
+    def all_crossed(p):
+        start, rows = pieces[p]
+        drain(wall.at[:, 0, pl.ds(start, rows)], crossing[p][1])
+
+    def wait_blocks(p, *ks):
+        start, rows = pieces[p]
+        for k in ks:
+            drain(wall.at[pl.ds(0, len(both(k))), 0, pl.ds(start, rows)], arriving[p][k])
+
+    def pass_on(p, j):
+        wait_blocks(p, strides[p] * j)
+        forward(p, j)
+        to_sibling(p, strides[p] * j)
+
+    def hand_over(p, *ks):
+        for k in ks:
+            wait_blocks(p, k)
+            to_sibling(p, k)
 
     def both(k):
-        return (k, -k) if k < 8 else (8,)
+        return (k, -k) if 0 < k < 8 else (k,)
 
     def relay(source, target, pair):
         sends, recvs = pair
@@ -253,14 +270,15 @@
         return sems.at[pl.ds(count[0] - 2, 2)]
 
     pair_a = two(), two()
+    forward(0, 0)
     relay(relayed, earr.at[x, y, d // 16], pair_a)
-    forward(0, 0)
+    forward(1, 0)
     f1 = gather1(feats, many)
-    forward(1, 0)
+    forward(2, 0)
     g1 = gather1(gins, many)
-    forward(2, 0)
-    to_sibling(0, 0, 64)
-    to_sibling(0, 64, 256)
+    for p in range(3):
+        to_sibling(p, 0)
+
     order = omap[...]
     source = order >> 4
     rank = (((source + d) & 15) << 5) + ((source >> 4) << 4) + (order & 15)
@@ -273,47 +291,32 @@
         (within < SHARD_ROWS) & ((p_iota >> 5) * SHARD_ROWS + within == e_iota), 1.0, 0.0
     ).astype(BF)
 
-    for p in range(3):
-        wait_blocks(p, 2)
-        forward(p, 1)
+    pass_on(0, 1)
+    hand_over(0, 1)
+    pass_on(1, 1)
+    pass_on(2, 1)
     relay_landed(relayed, lambda half: earr.at[x, y, half], pair_a)
     e1 = gather1(earr, many_e)
-    for i in both(2):
-        to_sibling(i, 0, 64)
-    for i in both(2):
-        to_sibling(i, 64, 256)
+    hand_over(1, 1)
     f2 = gather2(feats, f1)
-    for p in range(3):
-        wait_blocks(p, 4)
-        forward(p, 2)
+    hand_over(2, 1)
+    pass_on(0, 2)
+    hand_over(0, 3)
+    pass_on(1, 2)
     e2 = gather2(earr, e1)
     g2 = gather2(gins, g1)
-    for i in both(4):
-        to_sibling(i, 0, 64)
-    for i in both(4):
-        to_sibling(i, 64, 256)
-    for k in (1, 3):
-        wait_blocks(0, k)
-        for i in both(k):
-            to_sibling(i, 0, 64)
-    for p in range(3):
-        wait_blocks(p, 6)
-        forward(p, 3)
-    for i in both(6):
-        to_sibling(i, 0, 64)
-    for i in both(6):
-        to_sibling(i, 64, 256)
-    for k in (1, 3):
-        wait_blocks(1, k)
-        wait_blocks(2, k)
-        for i in both(k):
-            to_sibling(i, 64, 256)
-    for k in (5, 7, 8):
-        wait_blocks(0, k)
-        for i in both(k):
-            to_sibling(i, 0, 64)
-    all_crossed(0, 64)
-    landed(e2)
+    pass_on(2, 2)
+    hand_over(1, 3)
+    hand_over(2, 3)
+    pass_on(0, 3)
+    hand_over(0, 5)
+    pass_on(1, 3)
+    pass_on(2, 3)
+    hand_over(1, 5)
+    hand_over(0, 8)
+    hand_over(2, 5)
+    hand_over(0, 7)
+    all_crossed(0)
 
     padded = jnp.concatenate(
         [
@@ -323,6 +326,7 @@
         1,
     )
     kv_weight = dot(select, padded).astype(BF)
+    landed(e2)
     arrived = earr[...].reshape(512, ENC)
     kv_arrived = dot(arrived, kv_weight).astype(BF)
     kvs[256:768, :] = dot(spread_o, kv_arrived, 0, 0).astype(BF)
@@ -330,8 +334,10 @@
     finals.append((kvs.at[pl.ds(0, 256)], shift[0]))
     push(kvs.at[pl.ds(512, 256)], kvs.at[pl.ds(0, 256)], after, *shift)
 
-    landed(f2)
-    landed(g2)
+    hand_over(1, 8)
+    hand_over(2, 8)
+    hand_over(1, 7)
+    hand_over(2, 7)
 
     def block_of(a, i):
         return a[i // 4, i % 4].reshape(128, 256)
@@ -342,23 +348,12 @@
     def wo(i):
         return jnp.concatenate([wall[i, 0, 192:320, :], wall[i, 1, 192:320, :]], 1)
 
+    landed(f2)
+    all_crossed(1)
     queries = jnp.zeros((128, HDIM), F32)
-    d_att = jnp.zeros((128, HDIM), F32)
-    for k in (0, 2, 4, 6, 1, 3, 5, 7, 8):
-        if k in (5, 7, 8):
-            wait_blocks(1, k)
-            wait_blocks(2, k)
-            for i in both(k):
-                to_sibling(i, 64, 256)
-    all_crossed(64, 256)
-    for k in (0, 2, 4, 6, 1, 3, 5, 7, 8):
-        for dz in (0,) if k == 0 else both(k):
-            i = (z + dz + 16) % 16
-            queries += dot(block_of(feats, i), wq(i))
-            d_att += dot(block_of(gins, i), wo(i), 1, 1)
+    for i in range(16):
+        queries += dot(block_of(feats, i), wq(i))
     queries = queries.astype(BF)
-    d_att = d_att.astype(BF)
-
     drain(kvs.at[pl.ds(0, 256)], shift[1])
     keys = kvs[:, 0:HDIM]
     values = kvs[:, HDIM:]
@@ -374,6 +369,12 @@
     probs = expo / jnp.where(total > 0.0, total, 1.0)
     probs_half = probs.astype(BF)
     attended = dot(probs_half, values).astype(BF)
+    landed(g2)
+    all_crossed(2)
+    d_att = jnp.zeros((128, HDIM), F32)
+    for i in range(16):
+        d_att += dot(block_of(gins, i), wo(i), 1, 1)
+    d_att = d_att.astype(BF)
     grad_probs = dot(d_att, values, 1, 1)
     grad_scores = (
         probs * (grad_probs - jnp.sum(probs * grad_probs, -1, keepdims=True))
@@ -550,9 +551,15 @@
     layer_out, input_out, query_out, key_out, value_out, out_out, enc_out,
     held_l, held_i, held_q, held_p, held_o, held_e, sems,
 ):
-    pairs = [
-        (layer, held_l, layer_out),
-        (enc_g, held_e, enc_out),
+    pairs = []
+    for i in range(4):
+        for src, held, dst, rows in (
+            (layer, held_l, layer_out, 32),
+            (enc_g, held_e, enc_out, 128),
+        ):
+            span = pl.ds(rows * i, rows)
+            pairs.append((src.at[span], held.at[span], dst.at[span]))
+    pairs += [
         (input_g, held_i, input_out),
         (query_g, held_q, query_out),
         (out_g, held_o, out_out),
@@ -561,10 +568,10 @@
         pltpu.make_async_copy(src, held, sems.at[i]) for i, (src, held, _) in enumerate(pairs)
     ]
     outs = [
-        pltpu.make_async_copy(held, dst, sems.at[8 + i])
+        pltpu.make_async_copy(held, dst, sems.at[12 + i])
         for i, (_, held, dst) in enumerate(pairs)
     ]
-    pair_in = pltpu.make_async_copy(pair_g, held_p, sems.at[7])
+    pair_in = pltpu.make_async_copy(pair_g, held_p, sems.at[11])
     pair_in.start()
     for copy in ins:
         copy.start()
@@ -691,7 +698,7 @@
             pltpu.VMEM((32, 256), BF),
             pltpu.VMEM((128, 128), BF),
             pltpu.VMEM((512, ENC), BF),
-            pltpu.SemaphoreType.DMA((16,)),
+            pltpu.SemaphoreType.DMA((23,)),
         ],
         name="finish",
     )(*parts)

time: 93.7 us -> 93 us (level)
  no operation moved by 1% of the time
where the time goes in v3:
time: 93 us; the launch traced here: 92.8 us
  Pallas kernels  92.1 us (99%)
    pallas_call x1, Pallas kernels, shards(): pl.pallas_call(kernel, out_shape=outs, in_specs=[hbm] * 4 + [vmem] * 2 +...  89 us
    pallas_call x1, Pallas kernels, shards(): pl.pallas_call(finish, out_shape=[jax.ShapeDtypeStruct(shape, BF) for sha...  3.09 us

profile of v3, /device:TPU:1, one launch (start us, length us, event | category | flops | bytes accessed | tf_op | source)
XLA Modules:
  0.0 92.8 jit_solution(9885616193226067787)
XLA Ops:
  0.6 89.0 %retro.1 = (bf16[128,4096]{1,0:T(8,128)(2,1)}, bf16[128,256]{1,0:T(8,128)(2,1)}, bf16[128,128]{1,0:T(8,128)(2,1)}, bf16[32,256]{1,0:T(8,128)(2,1)}, bf16[128,128]{1,0:T(8,128)(2,1)}, /*index=5*/bf16[512,896]{1,0:T(8,128)(2,1)}) custom-call(bf16[128,256]{1,0:T(8,128)(2,1)} %tok.1, bf16[128,256]{1,0:T(8,128)(2,1)} %gout.1, bf16[128,128]{1,0:T(8,128)(2,1)} %qw.1, ...), custom_call_target="tpu_custom_call" | custom-call | tf_op jit(solution)/shard_map/retro/pallas_call | solution.py:659
  89.7 3.1 %finish.1 = (bf16[128,4096]{1,0:T(8,128)(2,1)}, bf16[128,256]{1,0:T(8,128)(2,1)}, bf16[128,128]{1,0:T(8,128)(2,1)}, bf16[28,128]{1,0:T(8,128)(2,1)}, bf16[28,128...) custom-call(bf16[128,4096]{1,0:T(8,128)(2,1)} %get-tuple-element.13.layer, ...), custom_call_target="tpu_custom_call" | custom-call | tf_op jit(solution)/shard_map/finish/pallas_call | solution.py:689
